TPU v7x, 32 devices: a whole 2x2x4 slice. The times are simulated.
32 devices in a mesh: ka: 2 (over x), gy: 4 (over z), gz: 4 (over y, core).
Axes of the slice: x: 2, y: 2, z: 4, core: 2. Of those that a mesh axis runs over, the one named last changes fastest.
Arguments:
- loads: float32 [32, 3, 128, 512], P('ka', None, 'gy', 'gz'), may hold values from -1 to 1
- sleeper_pos: int32 [32], P('ka'), may hold values from 0 to 127
- material: int32 [128, 512], P('gy', 'gz'), may hold values from 0 to 7, as said below
- material_table: float32 [8, 8], replicated, may hold values from -1 to 3, as said below
Outputs:
- adjoint_field: float32 [128, 2, 3, 128, 512], P('ka', None, None, 'gy', 'gz')
Inputs may be any that keep to these rules, and one draw needn't show every extreme that they name: layered: the material index never falls with depth in a column, layer boundaries vary from column to column, and every material occurs. `material_table`: shifts and damping positive, each material's coupling matrix diagonally dominant with a positive diagonal.
All inputs are finite; a program needn't handle non-finite values.
Results may differ from a plain program's by a relative error of at most 0.0002.
Values sent between devices are 32-bit elements; how exact they have to be, the bound alone decides.
No kernel may reach another device: no remote copies, remote signals or barrier semaphores. Data moves between devices by JAX's collectives and lax.ppermute only.
A program may use at most 128 MiB of HBM per device.

v0:
```python
import functools
import math

import jax
import jax.numpy as jnp
from jax import lax
from jax.experimental import pallas as pl
from jax.experimental.pallas import tpu as pltpu
from jax.sharding import PartitionSpec as P

KW = 128
NMAT = 8
DEG = 4
LANES = 128
HALF = 64
SEGS = 16
HY = 7
HB = 8


def spectral_bounds(material_table, squares):
    shifts = material_table[:, 0]
    diagonal_part = material_table[:, 1:4]
    off_diagonal = jnp.abs(material_table[:, 4:7])
    row_sums = jnp.stack(
        [
            off_diagonal[:, 0] + off_diagonal[:, 1],
            off_diagonal[:, 0] + off_diagonal[:, 2],
            off_diagonal[:, 1] + off_diagonal[:, 2],
        ],
        axis=1,
    )
    gersh_low = jnp.min(diagonal_part - row_sums, axis=1)
    gersh_high = jnp.max(diagonal_part + row_sums, axis=1)
    lowest = jnp.min(shifts[:, None] + gersh_low[:, None] * squares[None, :], axis=0)
    highest = 8.0 + jnp.max(shifts[:, None] + gersh_high[:, None] * squares[None, :], axis=0)
    return (lowest, highest)


def wave_squares(waves):
    return (2.0 * jnp.sin(waves.astype(jnp.float32) * (math.pi / KW))) ** 2


def phase_table(positions, waves):
    turn_index = positions[:, None] * waves[None, :] % KW
    angles = turn_index.astype(jnp.float32) * (2.0 * math.pi / KW)
    return (jnp.cos(angles), jnp.sin(angles))


def short(values):
    return lax.reduce_precision(values, exponent_bits=8, mantissa_bits=7)


def tables(positions, material_table, waves, width):
    count = waves.shape[0]
    squares = wave_squares(waves)
    lowest, highest = spectral_bounds(material_table, squares)
    center = 0.5 * (highest + lowest)
    half_width = 0.5 * (highest - lowest)
    ratio2 = (center / half_width) ** 2
    top = 8.0 * ratio2 * (ratio2 - 1.0) + 1.0
    h2 = half_width * half_width
    h4 = h2 * h2
    scale = 8.0 / (top * h4)
    scale = scale * scale

    cosines, sines = phase_table(positions, waves)
    phases = jnp.stack([cosines * scale, -sines * scale], axis=1)
    phases = jnp.pad(phases, ((0, 0), (0, 0), (0, HALF - count)))
    high = short(phases)
    low = short(phases - high)
    eye = jnp.eye(2, dtype=jnp.float32)
    three = jnp.eye(3, dtype=jnp.float32)
    spare = width - 3 * positions.shape[0]

    def blocks(table):
        wide = three[:, None, :, None, None] * table[None, :, None, :, :]
        wide = wide.reshape(3 * positions.shape[0], 6, HALF)
        wide = jnp.pad(wide, ((0, spare), (0, 0), (0, 0)))
        wide = eye[:, None, None, :, None] * wide[None, :, :, None, :]
        return wide.reshape(2 * width, 6 * LANES).astype(jnp.bfloat16)

    tw = jnp.concatenate([blocks(high), blocks(high), blocks(low)], axis=0)

    q = squares[None, :]
    entry = lambda column: material_table[:, column][:, None]
    fields = [center[None, :] - 4.0 - entry(0) - q * entry(c) for c in (1, 2, 3)]
    fields += [-q * entry(c) for c in (4, 5, 6)] + [q * entry(7)]
    fields = jnp.stack(fields, axis=1)
    fields = jnp.pad(fields, ((0, 0), (0, 0), (0, HALF - count)))
    first = short(fields)
    second = short(fields - first)
    third = short(fields - first - second)
    split = jnp.stack([first, second, third]).reshape(3 * NMAT, 7, HALF)
    split = jnp.pad(split, ((width - spare, spare - 3 * NMAT), (0, 0), (0, 0)))
    tc = eye[:, None, None, :, None] * split[None, :, :, None, :]
    tc = jnp.pad(tc.reshape(2 * width, 7 * LANES), ((0, 0), (0, LANES))).astype(jnp.bfloat16)

    vectors = jnp.stack([-h2, (top + 1.0) * h4 * 0.125, lowest * highest, center])
    vectors = jnp.pad(vectors, ((0, 0), (0, HALF - count)))
    vectors = jnp.broadcast_to(vectors[:, None, None, :], (4, 8, 2, HALF)).reshape(4, 8, LANES)
    return tw, tc, vectors


def lanes_for(sleepers):
    return -(-(3 * sleepers + 3 * NMAT) // LANES) * LANES


def two_parts(values):
    high = values.astype(jnp.bfloat16)
    low = (values - high.astype(jnp.float32)).astype(jnp.bfloat16)
    return high, low


def dot(a, b):
    return lax.dot_general(a, b, (((1,), (0,)), ((), ())), preferred_element_type=jnp.float32)


def dot_t(a, b):
    return lax.dot_general(a, b, (((1,), (1,)), ((), ())), preferred_element_type=jnp.float32)


def row_values(planes, row, height, sleepers, width):
    depth = planes.shape[1]
    parts = [planes[pl.ds(c * height + row, sleepers, stride=3 * height), :] for c in range(3)]
    material = planes[pl.ds(3 * sleepers * height + row, 1), :]
    number = lax.broadcasted_iota(jnp.int32, (width - 3 * sleepers, depth), 0)
    kind = jnp.where(number < 3 * NMAT, number % NMAT, -1).astype(jnp.float32)
    parts.append((kind == material).astype(jnp.float32))
    return jnp.concatenate(parts, axis=0)


def edge_kernel(sleepers, height, planes, out):
    depth = planes.shape[1]
    width = out.shape[2]
    spot = lax.broadcasted_iota(jnp.int32, (2 * HB, depth), 0)
    at = lax.broadcasted_iota(jnp.int32, (2 * HB, depth), 1)
    pick = (at == jnp.where(spot < HB, spot, spot + (depth - 2 * HB))).astype(jnp.bfloat16)

    def some_rows(block, carry):
        for line in range(8):
            row = 8 * block + line
            high, low = two_parts(row_values(planes, row, height, sleepers, width))
            out[row, :, :] = dot_t(pick, high) + dot_t(pick, low)
        return carry

    lax.fori_loop(0, height // 8, some_rows, 0)


def edges_of(planes, sleepers):
    height, depth = planes.shape[1:]
    return pl.pallas_call(
        functools.partial(edge_kernel, sleepers, height),
        out_shape=jax.ShapeDtypeStruct((height, 2 * HB, lanes_for(sleepers)), jnp.float32),
        in_specs=[pl.BlockSpec(memory_space=pltpu.VMEM)],
        out_specs=pl.BlockSpec(memory_space=pltpu.VMEM),
        compiler_params=pltpu.CompilerParams(vmem_limit_bytes=32 * 1024 * 1024),
        name="edge_columns",
    )(planes.reshape(-1, depth))


def field_kernel(
    sleepers, height, count, seglen,
    flags, planes, left, right, tw, tc, vectors, edge,
    out, source, coefs, a1, a2, a3, wide, b1, b2, turn, cells_of,
):
    depth = planes.shape[1]
    ny = height - 2 * HB
    width = left.shape[2]
    cells = 8 * seglen
    block = pl.program_id(0)
    out_rows = out.reshape(count * 48, depth)
    lane = lax.broadcasted_iota(jnp.int32, (8, LANES), 1)
    sub = lax.broadcasted_iota(jnp.int32, (8, LANES), 0)

    def at(zm):
        return pl.ds(8 * (zm + 1), 8)

    def store_ghosts(dst, slot, q, first, last):
        before = pltpu.roll(last, 1, 0)
        after = pltpu.roll(first, 7, 0)
        dst[slot, q, at(-1), :] = jnp.where(sub == 0, pltpu.roll(before, HALF, 1), before)
        dst[slot, q, at(seglen), :] = jnp.where(sub == 7, pltpu.roll(after, HALF, 1), after)

    def produce(first_row):
        halves = [[], []]
        for k in range(2):
            srow = first_row + k + (HB - HY)
            values = row_values(planes, srow, height, sleepers, width)
            for n in range(width // LANES):
                span = slice(n * LANES, (n + 1) * LANES)
                cells_of[k, n, HB : HB + depth, :] = jnp.transpose(values[span])
                cells_of[k, n, :HB, :] = left[srow, :, span]
                cells_of[k, n, HB + depth :, :] = right[srow, :, span]
        for k in range(2):
            for half in range(2):
                for zm in range(seglen):
                    spot = pl.ds(half * cells + zm, 8, stride=seglen)
                    pieces = [cells_of[k, n, spot, :] for n in range(width // LANES)]
                    halves[half].append(jnp.concatenate(pieces, axis=1))
        values = [jnp.concatenate(half, axis=0) for half in halves]
        parts = [two_parts(value) for value in values]
        high = jnp.concatenate([parts[0][0], parts[1][0]], axis=1)
        low = jnp.concatenate([parts[0][1], parts[1][1]], axis=1)
        three = jnp.concatenate([high, low, high], axis=1)
        for c in range(3):
            made = dot(three, tw[:, 2 * c * LANES : 2 * (c + 1) * LANES])
            for k in range(2):
                slot = (first_row + k) & 7
                for part in range(2):
                    q = part * 3 + c
                    plane = made[k * cells : (k + 1) * cells, part * LANES : (part + 1) * LANES]
                    source[slot, q, 8 : 8 + cells, :] = plane
                    store_ghosts(source, slot, q, plane[:8], plane[cells - 8 :])
        for f in range(0, 7, 2):
            made = dot(high, tc[:, f * LANES : (f + 2) * LANES])
            for k in range(2):
                slot = (first_row + k) & 15
                for g in range(f, min(f + 2, 7)):
                    coefs[slot, g, :, :] = made[
                        k * cells : (k + 1) * cells, (g - f) * LANES : (g - f + 1) * LANES
                    ]

    def apply(src, size, row, emit, shift=None, extra=None):
        slots = [(row + d) & (size - 1) for d in (-1, 0, 1, 2)]
        prev = [[src[slots[k + 1], q, at(-1), :] for q in range(6)] for k in range(2)]
        cur = [[src[slots[k + 1], q, at(0), :] for q in range(6)] for k in range(2)]
        for zm in range(seglen):
            nxt = [[src[slots[k + 1], q, at(zm + 1), :] for q in range(6)] for k in range(2)]
            for k in range(2):
                f = [coefs[(row + k) & 15, n, pl.ds(8 * zm, 8), :] for n in range(7)]
                diagonal = f[:3]
                if shift is not None:
                    diagonal = [d + shift for d in diagonal]
                matrix = (
                    (diagonal[0], f[3], f[4]),
                    (f[3], diagonal[1], f[5]),
                    (f[4], f[5], diagonal[2]),
                )
                results = []
                for q in range(6):
                    part, c = divmod(q, 3)
                    outer = src[slots[3 * k], q, at(zm), :]
                    near = (outer + cur[1 - k][q]) + (prev[k][q] + nxt[k][q])
                    mine = cur[k][3 * part : 3 * part + 3]
                    own = matrix[c][0] * mine[0] + matrix[c][1] * mine[1] + matrix[c][2] * mine[2]
                    damp = f[6] * cur[k][3 * (1 - part) + c]
                    total = near + own
                    total = total + damp if part == 0 else total - damp
                    if extra is not None:
                        other, other_size, weight = extra
                        slot = (row + k) & (other_size - 1)
                        total = total + weight * other[slot, q, at(zm), :]
                    results.append(total)
                emit(k, zm, results)
            prev, cur = cur, nxt

    def stage(src, size, dst, row, extra=None):
        ends = {}

        def emit(k, zm, results):
            if zm == HB - 1:
                results = [value * edge[0] for value in results]
            if zm == (HB + depth) % seglen:
                results = [value * edge[1] for value in results]
            for q in range(6):
                dst[(row + k) & 3, q, at(zm), :] = results[q]
            if zm in (0, seglen - 1):
                ends[k, zm] = results
            if zm == seglen - 1:
                for q in range(6):
                    store_ghosts(dst, (row + k) & 3, q, ends[k, 0][q], results[q])

        apply(src, size, row, emit, extra=extra)
        for k in range(2):
            spot = row + k
            outside = ((spot == HY - 1) & (flags[0] == 1)) | ((spot == HY + ny) & (flags[1] == 1))

            @pl.when(outside)
            def _():
                for q in range(6):
                    dst[spot & 3, q, :, :] = jnp.zeros(dst.shape[2:], jnp.float32)

    def finish(row, line):
        def emit(k, zm, results):
            for c in range(3):
                real, imag = results[c], results[3 + c]
                first = jnp.where(lane < HALF, real, pltpu.roll(imag, HALF, 1))
                second = jnp.where(lane < HALF, pltpu.roll(real, HALF, 1), imag)
                turn[3 * k + c, pl.ds(zm, 8, stride=seglen), :] = first
                turn[3 * k + c, pl.ds(cells + zm, 8, stride=seglen), :] = second

        apply(b2, 4, row, emit, shift=vectors[3])
        for k in range(2):
            for c in range(3):
                turned = jnp.transpose(turn[3 * k + c, HB : HB + depth, :])
                for part in range(2):
                    start = (part * 3 + c) * 8 + line + k
                    out_rows[pl.ds(start, count, stride=48), :] = turned[
                        part * HALF : part * HALF + count
                    ]

    def two_rows(pair, carry):
        base = 8 * block + 2 * pair - 2

        @pl.when(base >= 0)
        def _():
            produce(base)

        @pl.when(base >= 2)
        def _():
            stage(source, 8, a1, base - 1)

        @pl.when(base >= 4)
        def _():
            stage(a1, 4, a2, base - 2, (source, 8, vectors[0]))

        @pl.when(base >= 6)
        def _():
            stage(a2, 4, a3, base - 3)

        @pl.when(base >= 8)
        def _():
            stage(a3, 4, wide, base - 4, (source, 8, vectors[1]))

        @pl.when(base >= 10)
        def _():
            stage(wide, 4, b1, base - 5)

        @pl.when(base >= 12)
        def _():
            stage(b1, 4, b2, base - 6, (wide, 4, vectors[2]))

        @pl.when(base >= 14)
        def _():
            finish(base - 7, 2 * pair)

        return carry

    lax.fori_loop(0, 4, two_rows, 0)


def solve_field(flags, planes, left, right, tw, tc, vectors, edge, sleepers, count):
    height, depth = planes.shape[1:]
    width = left.shape[2]
    ny = height - 2 * HB
    seglen = (depth + 2 * HB) // SEGS
    blocks = ny // 8
    ring = lambda size: pltpu.VMEM((size, 6, 8 * (seglen + 2), LANES), jnp.float32)
    whole = pl.BlockSpec(memory_space=pltpu.VMEM)
    return pl.pallas_call(
        functools.partial(field_kernel, sleepers, height, count, seglen),
        grid=(blocks + 2,),
        out_shape=jax.ShapeDtypeStruct((count, 2, 3, ny, depth), jnp.float32),
        in_specs=[pl.BlockSpec(memory_space=pltpu.SMEM)] + [whole] * 7,
        out_specs=pl.BlockSpec(
            (count, 2, 3, 8, depth), lambda b: (0, 0, 0, jnp.maximum(b - 2, 0), 0)
        ),
        scratch_shapes=[
            ring(8),
            pltpu.VMEM((16, 7, 8 * seglen, LANES), jnp.float32),
            ring(4), ring(4), ring(4), ring(4), ring(4), ring(4),
            pltpu.VMEM((6, SEGS * seglen, LANES), jnp.float32),
            pltpu.VMEM((2, width // LANES, SEGS * seglen, LANES), jnp.float32),
        ],
        compiler_params=pltpu.CompilerParams(
            dimension_semantics=("arbitrary",), vmem_limit_bytes=56 * 1024 * 1024
        ),
        name="adjoint_field",
    )(flags, planes.reshape(-1, depth), left, right, tw, tc, vectors, edge)


def local(loads, sleeper_pos, material, material_table):
    ka = lax.axis_size("ka")
    gy, gz = lax.axis_size("gy"), lax.axis_size("gz")
    count = KW // ka
    waves = lax.axis_index("ka") * count + jnp.arange(count, dtype=jnp.int32)

    all_loads, all_pos = [loads], [sleeper_pos]
    for step in range(1, ka):
        turn = [(i, (i + step) % ka) for i in range(ka)]
        all_pos.append(lax.ppermute(sleeper_pos, "ka", turn))
        all_loads.append(lax.ppermute(loads, "ka", turn))
    positions = jnp.concatenate(all_pos)
    sleepers = positions.shape[0]
    ny, depth = material.shape
    planes = jnp.concatenate(
        [part.reshape(-1, ny, depth) for part in all_loads]
        + [material.astype(jnp.float32)[None]],
        axis=0,
    )

    def swap(low_part, high_part, axis, size):
        forward = [(i, i + 1) for i in range(size - 1)]
        backward = [(i + 1, i) for i in range(size - 1)]
        return lax.ppermute(high_part, axis, forward), lax.ppermute(low_part, axis, backward)

    above, below = swap(planes[:, :HB], planes[:, ny - HB :], "gy", gy)
    planes = jnp.concatenate([above, planes, below], axis=1)
    columns = edges_of(planes, sleepers)
    left, right = swap(columns[:, :HB], columns[:, HB:], "gz", gz)

    tw, tc, vectors = tables(positions, material_table, waves, lanes_for(sleepers))
    y_at, z_at = lax.axis_index("gy"), lax.axis_index("gz")
    flags = jnp.stack([y_at == 0, y_at == gy - 1]).astype(jnp.int32)
    sub = jnp.arange(8)[:, None]
    lane = jnp.arange(LANES)[None, :]
    edge = jnp.stack(
        [
            jnp.where((z_at == 0) & (sub == 0) & (lane < HALF), 0.0, 1.0),
            jnp.where((z_at == gz - 1) & (sub == 7) & (lane >= HALF), 0.0, 1.0),
        ]
    ).astype(jnp.float32)
    return solve_field(flags, planes, left, right, tw, tc, vectors, edge, sleepers, count)


def solution(mesh):
    return jax.shard_map(
        local,
        mesh=mesh,
        in_specs=(P("ka", None, "gy", "gz"), P("ka"), P("gy", "gz"), P()),
        out_specs=P("ka", None, None, "gy", "gz"),
        check_vma=False,
    )
```

profile of v0, /device:TPU:1, one launch (start us, length us, event | category | flops | bytes accessed | tf_op | source)
XLA Modules:
  0.0 112.2 jit_solution(13598267561667929133)
XLA Ops:
  0.0 2.0 %collective-permute-start.5 = (s32[16]{0:T(128)}, s32[16]{0:T(128)S(1)}, u32[]{:S(2)}, u32[]{:S(2)}) collective-permute-start(s32[16]{0:T(128)} %param.5), channel_id=1, source_target_pairs={{0,16},{16,0},{1,17},{17,1},{2,18},{18,2},{3,19},{19,3},{4,20},{20... | collective-permute-start | bytes 200 | tf_op jit(solution)/shard_map/ppermute | solution.py:382
  2.2 0.8 slice_abs_fusion
  3.0 1.3 %slice_reduce_fusion = (f32[8]{0:T(128)S(1)}, f32[8]{0:T(128)S(1)}, f32[8]{0:T(128)S(1)}, f32[8]{0:T(128)S(1)}, f32[8]{0:T(128)S(1)}, /*index=5*/f32[8]{0:T(128)S(1)}, f32[8]{0:T(128)S(1)}, f32[8]{0:T(128)S(1)}) fusion(f32[8,8]{1,0:T(8,128)} %param.7), kind=kLoop, calls=%fused_computation.45 | loop fusion | bytes 512 | tf_op jit(solution)/shard_map/slice | solution.py:86
  4.4 0.9 add_reduce_fusion.2
  6.0 0.1 copy.47
  6.1 0.1 pad.19.clone
  6.2 0.4 multiply_convert_fusion
  7.0 0.2 copy.44
  7.3 0.6 add_convert_fusion.flags
  8.0 0.6 pad_maximum_fusion.6.edge
  8.6 0.9 pad.20.tc
  9.5 10.8 %collective-permute-done = f32[16,3,32,128]{3,2,1,0:T(8,128)S(1)} collective-permute-done((f32[16,3,32,128]{3,2,1,0:T(8,128)}, f32[16,3,32,128]{3,2,1,0:T(8,128)S(1)}, u32[]{:S(2)}, u32[]{:S(2)}) %collective-permute-start) | collective-permute-done | bytes 786464 | tf_op jit(solution)/shard_map/ppermute | solution.py:383
  20.3 0.8 pad_maximum_fusion.4
  21.1 3.2 %collective-permute-start.1 = (f32[97,8,128]{2,1,0:T(8,128)}, f32[97,8,128]{2,1,0:T(8,128)S(1)}, u32[]{:S(2)}, u32[]{:S(2)}) collective-permute-start(f32[97,8,128]{2,1,0:T(8,128)} %get-tuple-element.19), channel_id=1, source_target_pairs={{0,4},{4,8},{8,12},{1,5},{5,9},{9,13},{2,6},{6,10},{10,14},{3,7},{... | collective-permute-start | bytes 1191944 | tf_op jit(solution)/shard_map/ppermute | solution.py:396
  24.4 1.3 %collective-permute-start.2 = (f32[97,8,128]{2,1,0:T(8,128)S(1)}, f32[97,8,128]{2,1,0:T(8,128)}, u32[]{:S(2)}, u32[]{:S(2)}) collective-permute-start(f32[97,8,128]{2,1,0:T(8,128)S(1)} %get-tuple-element.20), channel_id=1, source_target_pairs={{4,0},{8,4},{12,8},{5,1},{9,5},{13,9},{6,2},{10,6},{14,10},{7,3},{... | collective-permute-start | bytes 1191944 | tf_op jit(solution)/shard_map/ppermute | solution.py:396
  25.7 0.2 cosine_multiply_fusion
  25.9 0.1 broadcast_multiply_fusion.1
  26.1 0.1 copy.45
  26.2 0.1 copy.46
  26.4 4.9 %collective-permute-done.1 = f32[97,8,128]{2,1,0:T(8,128)S(1)} collective-permute-done((f32[97,8,128]{2,1,0:T(8,128)}, f32[97,8,128]{2,1,0:T(8,128)S(1)}, u32[]{:S(2)}, u32[]{:S(2)}) %collective-permute-start.1) | collective-permute-done | bytes 397344 | tf_op jit(solution)/shard_map/ppermute | solution.py:396
  31.3 3.6 %collective-permute-done.2 = f32[97,8,128]{2,1,0:T(8,128)} collective-permute-done((f32[97,8,128]{2,1,0:T(8,128)S(1)}, f32[97,8,128]{2,1,0:T(8,128)}, u32[]{:S(2)}, u32[]{:S(2)}) %collective-permute-start.2) | collective-permute-done | bytes 397344 | tf_op jit(solution)/shard_map/ppermute | solution.py:396
  34.9 1.2 %pad_maximum_fusion = f32[97,48,128]{2,1,0:T(8,128)S(1)} fusion(f32[97,8,128]{2,1,0:T(8,128)} %collective-permute-done.2, f32[1,32,128]{2,1,0:T(8,128)S(1)} %convert_bitcast_fusion, f32[48,32,128]{2,1,0:T(8,128)S(1)} %bitcast.84, f32[48,32,128]{2,1,0:T(8,128)S(1)} %bitcast.82, f32[97,8,128]{2,1,0:T(8,128)S(1)} %collective-permute-done.1), kind=kLoop, calls=%fused_computation | loop fusion | flops 2383872 | bytes 4767744 | tf_op jit(solution)/shard_map/concatenate | solution.py:399
  36.1 2.4 %edge_columns.1 = f32[48,16,128]{2,1,0:T(8,128)S(1)} custom-call(f32[4656,128]{1,0:T(8,128)S(1)} %bitcast.79), custom_call_target="tpu_custom_call" | custom-call | tf_op jit(solution)/shard_map/edge_columns/pallas_call | solution.py:152
  38.5 5.0 %collective-permute-start.4 = (f32[48,8,128]{2,1,0:T(8,128)S(1)}, f32[48,8,128]{2,1,0:T(8,128)S(1)}, u32[]{:S(2)}, u32[]{:S(2)}) collective-permute-start(f32[48,8,128]{2,1,0:T(8,128)S(1)} %get-tuple-element.21), channel_id=1, source_target_pairs={{1,0},{2,1},{3,2},{5,4},{6,5},{7,6},{9,8},{10,9},{11,10},{13,12},{... | collective-permute-start | bytes 589832 | tf_op jit(solution)/shard_map/ppermute | solution.py:396
  43.5 3.0 %collective-permute-start.3 = (f32[48,8,128]{2,1,0:T(8,128)S(1)}, f32[48,8,128]{2,1,0:T(8,128)S(1)}, u32[]{:S(2)}, u32[]{:S(2)}) collective-permute-start(f32[48,8,128]{2,1,0:T(8,128)S(1)} %get-tuple-element.22), channel_id=1, source_target_pairs={{0,1},{1,2},{2,3},{4,5},{5,6},{6,7},{8,9},{9,10},{10,11},{12,13},{... | collective-permute-start | bytes 589832 | tf_op jit(solution)/shard_map/ppermute | solution.py:396
  46.6 0.6 multiply_convert_fusion.2
  47.2 0.2 copy.35
  47.5 0.2 copy.37
  47.6 1.1 pad_maximum_fusion.1.tw
  48.8 0.4 collective-permute-done.3.left
  49.2 0.6 broadcast_in_dim.19.vectors
  49.8 62.4 %adjoint_field.1 = f32[64,2,3,32,128]{4,3,2,1,0:T(8,128)} custom-call(s32[2]{0:T(128)} %add_convert_fusion.flags, f32[4656,128]{1,0:T(8,128)} %bitcast.80, f32[48,8,128]{2,1,0:T(8,128)} %copy-done.3, f32[48,8,128]{2,1,0:T(8,128)} %copy-done.2, bf16[768,768]{1,0:T(8,128)(2,1)} %pad_maximum_fusion.1.tw, bf16[256,1024]{1,0:T(8,128)(2,1)} %pad.20.tc, ...), custom_call_target="tpu_custom_call" | custom-call | tf_op jit(solution)/shard_map/adjoint_field/pallas_call | solution.py:351
  (53 shorter events, 1.7 us)
Async XLA Ops:
  0.0 8.6 %copy-start.4 = (s32[32,128]{1,0:T(8,128)S(1)}, s32[32,128]{1,0:T(8,128)}, u32[]{:S(2)}) copy-start(s32[32,128]{1,0:T(8,128)} %param.6) | copy-start | bytes 49156
  0.0 9.4 %collective-permute-start.5 = (s32[16]{0:T(128)}, s32[16]{0:T(128)S(1)}, u32[]{:S(2)}, u32[]{:S(2)}) collective-permute-start(s32[16]{0:T(128)} %param.5), channel_id=1, source_target_pairs={{0,16},{16,0},{1,17},{17,1},{2,18},{18,2},{3,19},{19,3},{4,20},{20... | collective-permute-start | bytes 200 | tf_op jit(solution)/shard_map/ppermute | solution.py:382
  2.0 18.3 %collective-permute-start = (f32[16,3,32,128]{3,2,1,0:T(8,128)}, f32[16,3,32,128]{3,2,1,0:T(8,128)S(1)}, u32[]{:S(2)}, u32[]{:S(2)}) collective-permute-start(f32[16,3,32,128]{3,2,1,0:T(8,128)} %param.4), channel_id=1, source_target_pairs={{0,16},{16,0},{1,17},{17,1},{2,18},{18,2},{3,19},{19,3},{4,20},{20... | collective-permute-start | bytes 2359304 | tf_op jit(solution)/shard_map/ppermute | solution.py:383
  5.4 4.1 %copy-start.5 = (s32[16]{0:T(128)S(1)}, s32[16]{0:T(128)}, u32[]{:S(2)}) copy-start(s32[16]{0:T(128)} %param.5) | copy-start | bytes 196
  5.4 14.9 %copy-start.1 = (f32[16,3,32,128]{3,2,1,0:T(8,128)S(1)}, f32[16,3,32,128]{3,2,1,0:T(8,128)}, u32[]{:S(2)}) copy-start(f32[16,3,32,128]{3,2,1,0:T(8,128)} %param.4) | copy-start | bytes 2359300
  21.1 10.1 %collective-permute-start.1 = (f32[97,8,128]{2,1,0:T(8,128)}, f32[97,8,128]{2,1,0:T(8,128)S(1)}, u32[]{:S(2)}, u32[]{:S(2)}) collective-permute-start(f32[97,8,128]{2,1,0:T(8,128)} %get-tuple-element.19), channel_id=1, source_target_pairs={{0,4},{4,8},{8,12},{1,5},{5,9},{9,13},{2,6},{6,10},{10,14},{3,7},{... | collective-permute-start | bytes 1191944 | tf_op jit(solution)/shard_map/ppermute | solution.py:396
  24.4 10.6 %collective-permute-start.2 = (f32[97,8,128]{2,1,0:T(8,128)S(1)}, f32[97,8,128]{2,1,0:T(8,128)}, u32[]{:S(2)}, u32[]{:S(2)}) collective-permute-start(f32[97,8,128]{2,1,0:T(8,128)S(1)} %get-tuple-element.20), channel_id=1, source_target_pairs={{4,0},{8,4},{12,8},{5,1},{9,5},{13,9},{6,2},{10,6},{14,10},{7,3},{... | collective-permute-start | bytes 1191944 | tf_op jit(solution)/shard_map/ppermute | solution.py:396
  36.1 11.1 %copy-start = (f32[97,48,128]{2,1,0:T(8,128)}, f32[97,48,128]{2,1,0:T(8,128)S(1)}, u32[]{:S(2)}) copy-start(f32[97,48,128]{2,1,0:T(8,128)S(1)} %pad_maximum_fusion) | copy-start | bytes 7151620
  38.5 10.2 %collective-permute-start.4 = (f32[48,8,128]{2,1,0:T(8,128)S(1)}, f32[48,8,128]{2,1,0:T(8,128)S(1)}, u32[]{:S(2)}, u32[]{:S(2)}) collective-permute-start(f32[48,8,128]{2,1,0:T(8,128)S(1)} %get-tuple-element.21), channel_id=1, source_target_pairs={{1,0},{2,1},{3,2},{5,4},{6,5},{7,6},{9,8},{10,9},{11,10},{13,12},{... | collective-permute-start | bytes 589832 | tf_op jit(solution)/shard_map/ppermute | solution.py:396
  43.5 5.6 %collective-permute-start.3 = (f32[48,8,128]{2,1,0:T(8,128)S(1)}, f32[48,8,128]{2,1,0:T(8,128)S(1)}, u32[]{:S(2)}, u32[]{:S(2)}) collective-permute-start(f32[48,8,128]{2,1,0:T(8,128)S(1)} %get-tuple-element.22), channel_id=1, source_target_pairs={{0,1},{1,2},{2,3},{4,5},{5,6},{6,7},{8,9},{9,10},{10,11},{12,13},{... | collective-permute-start | bytes 589832 | tf_op jit(solution)/shard_map/ppermute | solution.py:396
  48.8 1.0 copy-start.2
  49.2 0.7 copy-start.3
where the time goes:
time: 113 us; the launch traced here: 112 us
  Pallas kernels  64.7 us (57%)
  waiting for transfers between devices  19.8 us (18%)
  starting transfers between devices  14.6 us (13%)
  other arithmetic  8.27 us (7%)
  local copies, waits for them, and re-layouts  4.46 us (4%)
    pallas_call x1, Pallas kernels, solve_field(): pl.pallas_call(functools.partial(field_kernel, sleepers, height, count, s...  62.4 us
    ppermute x1, waiting for transfers between devices, local(): all_loads.append(lax.ppermute(loads, 'ka', turn))  10.8 us
    ppermute x2, starting transfers between devices, swap(): lax.ppermute(low_part, axis, backward)  6.27 us
    ppermute x2, starting transfers between devices, swap(): lax.ppermute(high_part, axis, forward)  6.26 us
    ppermute x2, waiting for transfers between devices, swap(): lax.ppermute(high_part, axis, forward)  5.29 us
    ppermute x2, waiting for transfers between devices, swap(): lax.ppermute(low_part, axis, backward)  3.65 us
    pallas_call x1, Pallas kernels, edges_of(): pl.pallas_call(functools.partial(edge_kernel, sleepers, height), out_shap...  2.38 us
  transfers between devices with their start and end apart: 6, of which 4 were waited for; matrix products, arithmetic and copies ran while one was open for 9% of the time, Pallas kernels for 0%

commit v1 on v0

v1 whole, which is shorter than its diff:
```python
import functools
import math

import jax
import jax.numpy as jnp
from jax import lax
from jax.experimental import pallas as pl
from jax.experimental.pallas import tpu as pltpu
from jax.sharding import PartitionSpec as P

KW = 128
NMAT = 8
DEG = 4
LANES = 128
HALF = 64
SEGS = 16
HY = 7
HB = 8


def spectral_bounds(material_table, squares):
    shifts = material_table[:, 0]
    diagonal_part = material_table[:, 1:4]
    off_diagonal = jnp.abs(material_table[:, 4:7])
    row_sums = jnp.stack(
        [
            off_diagonal[:, 0] + off_diagonal[:, 1],
            off_diagonal[:, 0] + off_diagonal[:, 2],
            off_diagonal[:, 1] + off_diagonal[:, 2],
        ],
        axis=1,
    )
    gersh_low = jnp.min(diagonal_part - row_sums, axis=1)
    gersh_high = jnp.max(diagonal_part + row_sums, axis=1)
    lowest = jnp.min(shifts[:, None] + gersh_low[:, None] * squares[None, :], axis=0)
    highest = 8.0 + jnp.max(shifts[:, None] + gersh_high[:, None] * squares[None, :], axis=0)
    return (lowest, highest)


def wave_squares(waves):
    return (2.0 * jnp.sin(waves.astype(jnp.float32) * (math.pi / KW))) ** 2


def phase_table(positions, waves):
    turn_index = positions[:, None] * waves[None, :] % KW
    angles = turn_index.astype(jnp.float32) * (2.0 * math.pi / KW)
    return (jnp.cos(angles), jnp.sin(angles))


def short(values):
    return lax.reduce_precision(values, exponent_bits=8, mantissa_bits=7)


def tables(positions, material_table, waves, width):
    count = waves.shape[0]
    squares = wave_squares(waves)
    lowest, highest = spectral_bounds(material_table, squares)
    center = 0.5 * (highest + lowest)
    half_width = 0.5 * (highest - lowest)
    ratio2 = (center / half_width) ** 2
    top = 8.0 * ratio2 * (ratio2 - 1.0) + 1.0
    h2 = half_width * half_width
    h4 = h2 * h2
    scale = 8.0 / (top * h4)
    scale = scale * scale

    cosines, sines = phase_table(positions, waves)
    phases = jnp.stack([cosines * scale, -sines * scale], axis=1)
    phases = jnp.pad(phases, ((0, 0), (0, 0), (0, HALF - count)))
    high = short(phases)
    low = short(phases - high)
    eye = jnp.eye(2, dtype=jnp.float32)
    three = jnp.eye(3, dtype=jnp.float32)
    spare = width - 3 * positions.shape[0]

    def blocks(table):
        wide = three[:, None, :, None, None] * table[None, :, None, :, :]
        wide = wide.reshape(3 * positions.shape[0], 6, HALF)
        wide = jnp.pad(wide, ((0, spare), (0, 0), (0, 0)))
        wide = eye[:, None, None, :, None] * wide[None, :, :, None, :]
        return wide.reshape(2 * width, 6 * LANES).astype(jnp.bfloat16)

    tw = jnp.concatenate([blocks(high), blocks(high), blocks(low)], axis=0)

    q = squares[None, :]
    entry = lambda column: material_table[:, column][:, None]
    fields = [center[None, :] - 4.0 - entry(0) - q * entry(c) for c in (1, 2, 3)]
    fields += [-q * entry(c) for c in (4, 5, 6)] + [q * entry(7)]
    fields = jnp.stack(fields, axis=1)
    fields = jnp.pad(fields, ((0, 0), (0, 0), (0, HALF - count)))
    first = short(fields)
    second = short(fields - first)
    third = short(fields - first - second)
    split = jnp.stack([first, second, third]).reshape(3 * NMAT, 7, HALF)
    split = jnp.pad(split, ((width - spare, spare - 3 * NMAT), (0, 0), (0, 0)))
    tc = eye[:, None, None, :, None] * split[None, :, :, None, :]
    tc = jnp.pad(tc.reshape(2 * width, 7 * LANES), ((0, 0), (0, LANES))).astype(jnp.bfloat16)

    vectors = jnp.stack([-h2, (top + 1.0) * h4 * 0.125, lowest * highest, center])
    vectors = jnp.pad(vectors, ((0, 0), (0, HALF - count)))
    vectors = jnp.broadcast_to(vectors[:, None, None, :], (4, 8, 2, HALF)).reshape(4, 8, LANES)
    return tw, tc, vectors


def lanes_for(sleepers):
    return -(-(3 * sleepers + 3 * NMAT) // LANES) * LANES


def two_parts(values):
    high = values.astype(jnp.bfloat16)
    low = (values - high.astype(jnp.float32)).astype(jnp.bfloat16)
    return high, low


def dot(a, b):
    return lax.dot_general(a, b, (((1,), (0,)), ((), ())), preferred_element_type=jnp.float32)


def dot_t(a, b):
    return lax.dot_general(a, b, (((1,), (1,)), ((), ())), preferred_element_type=jnp.float32)


def row_values(planes, row, height, sleepers, width):
    depth = planes.shape[1]
    parts = [planes[pl.ds(c * height + row, sleepers, stride=3 * height), :] for c in range(3)]
    material = planes[pl.ds(3 * sleepers * height + row, 1), :]
    number = lax.broadcasted_iota(jnp.int32, (width - 3 * sleepers, depth), 0)
    kind = jnp.where(number < 3 * NMAT, number % NMAT, -1).astype(jnp.float32)
    parts.append((kind == material).astype(jnp.float32))
    return jnp.concatenate(parts, axis=0)


def gather(spots, pieces, planes, sems):
    copies = []
    for n, (piece, first, count, plane, row, target) in enumerate(spots):
        src = pieces[piece]
        copies.append(
            pltpu.make_async_copy(
                src.at[plane : plane + count, row[0] : row[0] + row[1], :],
                planes.at[first : first + count, target : target + row[1], :],
                sems.at[n],
            )
        )
    for copy in copies:
        copy.start()
    for copy in copies:
        copy.wait()


def edge_kernel(sleepers, spots, *refs):
    *pieces, out, planes, sems = refs
    gather(spots, pieces, planes, sems)
    height, depth = planes.shape[1:]
    width = out.shape[2]
    spot = lax.broadcasted_iota(jnp.int32, (2 * HB, depth), 0)
    at = lax.broadcasted_iota(jnp.int32, (2 * HB, depth), 1)
    pick = (at == jnp.where(spot < HB, spot, spot + (depth - 2 * HB))).astype(jnp.bfloat16)
    flat = planes.reshape(planes.shape[0] * height, depth)

    def some_rows(block, carry):
        for line in range(8):
            row = 8 * block + line
            high, low = two_parts(row_values(flat, row, height, sleepers, width))
            out[row, :, :] = dot_t(pick, high) + dot_t(pick, low)
        return carry

    lax.fori_loop(0, height // 8, some_rows, 0)


def edges_of(spots, pieces, sleepers, height, depth):
    return pl.pallas_call(
        functools.partial(edge_kernel, sleepers, spots),
        out_shape=jax.ShapeDtypeStruct((height, 2 * HB, lanes_for(sleepers)), jnp.float32),
        in_specs=[pl.BlockSpec(memory_space=pl.ANY)] * len(pieces),
        out_specs=pl.BlockSpec(memory_space=pltpu.VMEM),
        scratch_shapes=[
            pltpu.VMEM((3 * sleepers + 1, height, depth), jnp.float32),
            pltpu.SemaphoreType.DMA((len(spots),)),
        ],
        compiler_params=pltpu.CompilerParams(vmem_limit_bytes=32 * 1024 * 1024),
        name="edge_columns",
    )(*pieces)


def field_kernel(sleepers, count, seglen, spots, *refs):
    flags, left, right, tw, tc, vectors, edge, *pieces = refs[: 7 + len(refs) - 21]
    (out, planes, sems, source, ghosts, coefs, lhs,
     a1, a2, a3, wide, b1, b2, turn) = refs[7 + len(refs) - 21 :]
    height, depth = planes.shape[1:]
    flat = planes.reshape(planes.shape[0] * height, depth)
    ny = height - 2 * HB
    width = left.shape[2]
    cells = 8 * seglen
    block = pl.program_id(0)
    out_rows = out.reshape(count * 48, depth)
    lane = lax.broadcasted_iota(jnp.int32, (8, LANES), 1)
    sub = lax.broadcasted_iota(jnp.int32, (8, LANES), 0)

    @pl.when(block == 0)
    def _():
        gather(spots, pieces, planes, sems)

    def at(zm):
        return pl.ds(8 * (zm + 1), 8)

    def around(first, last):
        before = pltpu.roll(last, 1, 0)
        after = pltpu.roll(first, 7, 0)
        return (
            jnp.where(sub == 0, pltpu.roll(before, HALF, 1), before),
            jnp.where(sub == 7, pltpu.roll(after, HALF, 1), after),
        )

    def store_ghosts(dst, slot, q, first, last):
        dst[slot, q, at(-1), :], dst[slot, q, at(seglen), :] = around(first, last)

    def line_at(row, zm):
        return pl.ds(pl.multiple_of(((row + 2) & 15) * cells, 8) + 8 * zm, 8)

    def column(q):
        part, c = divmod(q, 3)
        return slice((2 * c + part) * LANES, (2 * c + part + 1) * LANES)

    def read_source(row, q, zm):
        if zm == -1:
            return ghosts[(row + 2) & 15, q, :8, :]
        if zm == seglen:
            return ghosts[(row + 2) & 15, q, 8:, :]
        return source[line_at(row, zm), column(q)]

    def reader(ring):
        return lambda row, q, zm: ring[row & 3, q, at(zm), :]

    def produce():
        chunks = width // LANES
        for line in range(8):
            srow = jnp.maximum(8 * block + line - 2 + (HB - HY), 0)
            values = row_values(flat, srow, height, sleepers, width)
            for n in range(chunks):
                span = slice(n * LANES, (n + 1) * LANES)
                turn[line * chunks + n, HB : HB + depth, :] = jnp.transpose(values[span])
                turn[line * chunks + n, :HB, :] = left[srow, :, span]
                turn[line * chunks + n, HB + depth :, :] = right[srow, :, span]
        for pair in range(4):
            halves = [[], []]
            for line in (2 * pair, 2 * pair + 1):
                for half in range(2):
                    for zm in range(seglen):
                        spot = pl.ds(half * cells + zm, 8, stride=seglen)
                        pieces_at = [turn[line * chunks + n, spot, :] for n in range(chunks)]
                        halves[half].append(jnp.concatenate(pieces_at, axis=1))
            values = jnp.concatenate(
                [jnp.concatenate(half, axis=0) for half in halves], axis=1
            )
            high, low = two_parts(values)
            rows = slice(2 * pair * cells, 2 * (pair + 1) * cells)
            lhs[rows, : 2 * width] = high
            lhs[rows, 2 * width : 4 * width] = low
            lhs[rows, 4 * width :] = high
        target = pl.ds(pl.multiple_of((block & 1) * (8 * cells), 8), 8 * cells)
        for c in range(3):
            span = slice(2 * c * LANES, 2 * (c + 1) * LANES)
            source[target, span] = dot(lhs[...], tw[:, span])
        for f in range(0, 8, 2):
            span = slice(f * LANES, (f + 2) * LANES)
            coefs[target, span] = dot(lhs[:, : 2 * width], tc[:, span])
        for line in range(8):
            row = 8 * block - 2 + line
            for q in range(6):
                first = read_source(row, q, 0)
                last = read_source(row, q, seglen - 1)
                ghosts[(row + 2) & 15, q, :8, :], ghosts[(row + 2) & 15, q, 8:, :] = around(
                    first, last
                )

    def apply(src, row, emit, shift=None, extra=None):
        prev = [[src(row + k, q, -1) for q in range(6)] for k in range(2)]
        cur = [[src(row + k, q, 0) for q in range(6)] for k in range(2)]
        for zm in range(seglen):
            nxt = [[src(row + k, q, zm + 1) for q in range(6)] for k in range(2)]
            for k in range(2):
                f = [
                    coefs[line_at(row + k, zm), n * LANES : (n + 1) * LANES] for n in range(7)
                ]
                diagonal = f[:3]
                if shift is not None:
                    diagonal = [d + shift for d in diagonal]
                matrix = (
                    (diagonal[0], f[3], f[4]),
                    (f[3], diagonal[1], f[5]),
                    (f[4], f[5], diagonal[2]),
                )
                results = []
                for q in range(6):
                    part, c = divmod(q, 3)
                    outer = src(row + 3 * k - 1, q, zm)
                    near = (outer + cur[1 - k][q]) + (prev[k][q] + nxt[k][q])
                    mine = cur[k][3 * part : 3 * part + 3]
                    own = matrix[c][0] * mine[0] + matrix[c][1] * mine[1] + matrix[c][2] * mine[2]
                    damp = f[6] * cur[k][3 * (1 - part) + c]
                    total = near + own
                    total = total + damp if part == 0 else total - damp
                    if extra is not None:
                        other, weight = extra
                        total = total + weight * other(row + k, q, zm)
                    results.append(total)
                emit(k, zm, results)
            prev, cur = cur, nxt

    def stage(src, dst, row, extra=None):
        ends = {}

        def emit(k, zm, results):
            if zm == HB - 1:
                results = [value * edge[0] for value in results]
            if zm == (HB + depth) % seglen:
                results = [value * edge[1] for value in results]
            for q in range(6):
                dst[(row + k) & 3, q, at(zm), :] = results[q]
            if zm in (0, seglen - 1):
                ends[k, zm] = results
            if zm == seglen - 1:
                for q in range(6):
                    store_ghosts(dst, (row + k) & 3, q, ends[k, 0][q], results[q])

        apply(src, row, emit, extra=extra)
        for k in range(2):
            spot = row + k
            outside = ((spot == HY - 1) & (flags[0] == 1)) | ((spot == HY + ny) & (flags[1] == 1))

            @pl.when(outside)
            def _():
                for q in range(6):
                    dst[spot & 3, q, :, :] = jnp.zeros(dst.shape[2:], jnp.float32)

    def finish(row, line):
        def emit(k, zm, results):
            for c in range(3):
                real, imag = results[c], results[3 + c]
                first = jnp.where(lane < HALF, real, pltpu.roll(imag, HALF, 1))
                second = jnp.where(lane < HALF, pltpu.roll(real, HALF, 1), imag)
                turn[3 * k + c, pl.ds(zm, 8, stride=seglen), :] = first
                turn[3 * k + c, pl.ds(cells + zm, 8, stride=seglen), :] = second

        apply(reader(b2), row, emit, shift=vectors[3])
        for k in range(2):
            for c in range(3):
                turned = jnp.transpose(turn[3 * k + c, HB : HB + depth, :])
                for part in range(2):
                    start = (part * 3 + c) * 8 + line + k
                    out_rows[pl.ds(start, count, stride=48), :] = turned[
                        part * HALF : part * HALF + count
                    ]

    def two_rows(pair, carry):
        base = 8 * block + 2 * pair - 2

        @pl.when(base >= 2)
        def _():
            stage(read_source, a1, base - 1)

        @pl.when(base >= 4)
        def _():
            stage(reader(a1), a2, base - 2, (read_source, vectors[0]))

        @pl.when(base >= 6)
        def _():
            stage(reader(a2), a3, base - 3)

        @pl.when(base >= 8)
        def _():
            stage(reader(a3), wide, base - 4, (read_source, vectors[1]))

        @pl.when(base >= 10)
        def _():
            stage(reader(wide), b1, base - 5)

        @pl.when(base >= 12)
        def _():
            stage(reader(b1), b2, base - 6, (reader(wide), vectors[2]))

        @pl.when(base >= 14)
        def _():
            finish(base - 7, 2 * pair)

        return carry

    produce()
    lax.fori_loop(0, 4, two_rows, 0)


def solve_field(spots, pieces, flags, left, right, tw, tc, vectors, edge, sleepers, count):
    height, _, width = left.shape
    depth = pieces[0].shape[2]
    ny = height - 2 * HB
    seglen = (depth + 2 * HB) // SEGS
    blocks = ny // 8
    ring = pltpu.VMEM((4, 6, 8 * (seglen + 2), LANES), jnp.float32)
    whole = pl.BlockSpec(memory_space=pltpu.VMEM)
    return pl.pallas_call(
        functools.partial(field_kernel, sleepers, count, seglen, spots),
        grid=(blocks + 2,),
        out_shape=jax.ShapeDtypeStruct((count, 2, 3, ny, depth), jnp.float32),
        in_specs=[pl.BlockSpec(memory_space=pltpu.SMEM)]
        + [whole] * 6
        + [pl.BlockSpec(memory_space=pl.ANY)] * len(pieces),
        out_specs=pl.BlockSpec(
            (count, 2, 3, 8, depth), lambda b: (0, 0, 0, jnp.maximum(b - 2, 0), 0)
        ),
        scratch_shapes=[
            pltpu.VMEM((3 * sleepers + 1, height, depth), jnp.float32),
            pltpu.SemaphoreType.DMA((len(spots),)),
            pltpu.VMEM((16 * 8 * seglen, 6 * LANES), jnp.float32),
            pltpu.VMEM((16, 6, 16, LANES), jnp.float32),
            pltpu.VMEM((16 * 8 * seglen, 8 * LANES), jnp.float32),
            pltpu.VMEM((8 * 8 * seglen, 6 * width), jnp.bfloat16),
            ring, ring, ring, ring, ring, ring,
            pltpu.VMEM((max(8 * (width // LANES), 6), SEGS * seglen, LANES), jnp.float32),
        ],
        compiler_params=pltpu.CompilerParams(
            dimension_semantics=("arbitrary",), vmem_limit_bytes=56 * 1024 * 1024
        ),
        name="adjoint_field",
    )(flags, left, right, tw, tc, vectors, edge, *pieces)


def local(loads, sleeper_pos, material, material_table):
    ka = lax.axis_size("ka")
    gy, gz = lax.axis_size("gy"), lax.axis_size("gz")
    count = KW // ka
    waves = lax.axis_index("ka") * count + jnp.arange(count, dtype=jnp.int32)
    sleepers = ka * loads.shape[0]
    own = 3 * loads.shape[0]
    ny, depth = material.shape
    height = ny + 2 * HB
    loads = loads.reshape(own, ny, depth)
    material = material.astype(jnp.float32)[None]

    def shift(array, axis, size, by):
        pairs = [(i, i + by) for i in range(size) if 0 <= i + by < size]
        return lax.ppermute(array, axis, pairs)

    turns = [[(i, (i + step) % ka) for i in range(ka)] for step in range(1, ka)]
    ends = jnp.concatenate([loads[:, :HB], loads[:, ny - HB :]], axis=1)
    got_ends = [lax.ppermute(ends, "ka", turn) for turn in turns]
    inner = loads[:, HB : ny - HB]
    got_inner = [lax.ppermute(inner, "ka", turn) for turn in turns]
    all_pos = [sleeper_pos] + [lax.ppermute(sleeper_pos, "ka", turn) for turn in turns]
    low = jnp.concatenate([loads[:, :HB], material[:, :HB]], axis=0)
    high = jnp.concatenate([loads[:, ny - HB :], material[:, ny - HB :]], axis=0)
    above, below = shift(high, "gy", gy, 1), shift(low, "gy", gy, -1)

    pieces = [loads, material, above, below]
    spots = [
        (0, 0, own, 0, (0, ny), HB),
        (1, 3 * sleepers, 1, 0, (0, ny), HB),
        (2, 0, own, 0, (0, HB), 0),
        (2, 3 * sleepers, 1, own, (0, HB), 0),
        (3, 0, own, 0, (0, HB), HB + ny),
        (3, 3 * sleepers, 1, own, (0, HB), HB + ny),
    ]
    for step, (outer, middle) in enumerate(zip(got_ends, got_inner)):
        first = own * (step + 1)
        number = len(pieces)
        pieces += [
            outer,
            middle,
            shift(outer[:, HB:], "gy", gy, 1),
            shift(outer[:, :HB], "gy", gy, -1),
        ]
        spots += [
            (number, first, own, 0, (0, HB), HB),
            (number, first, own, 0, (HB, HB), ny),
            (number + 1, first, own, 0, (0, ny - 2 * HB), 2 * HB),
            (number + 2, first, own, 0, (0, HB), 0),
            (number + 3, first, own, 0, (0, HB), HB + ny),
        ]

    tw, tc, vectors = tables(
        jnp.concatenate(all_pos), material_table, waves, lanes_for(sleepers)
    )
    y_at, z_at = lax.axis_index("gy"), lax.axis_index("gz")
    flags = jnp.stack([y_at == 0, y_at == gy - 1]).astype(jnp.int32)
    sub = jnp.arange(8)[:, None]
    lane = jnp.arange(LANES)[None, :]
    edge = jnp.stack(
        [
            jnp.where((z_at == 0) & (sub == 0) & (lane < HALF), 0.0, 1.0),
            jnp.where((z_at == gz - 1) & (sub == 7) & (lane >= HALF), 0.0, 1.0),
        ]
    ).astype(jnp.float32)
    tied = lax.optimization_barrier((pieces[-1], tw, tc, vectors, flags, edge))
    pieces[-1], tw, tc, vectors, flags, edge = tied

    columns = edges_of(spots, pieces, sleepers, height, depth)
    left = shift(columns[:, HB:], "gz", gz, 1)
    right = shift(columns[:, :HB], "gz", gz, -1)
    return solve_field(
        spots, pieces, flags, left, right, tw, tc, vectors, edge, sleepers, count
    )


def solution(mesh):
    return jax.shard_map(
        local,
        mesh=mesh,
        in_specs=(P("ka", None, "gy", "gz"), P("ka"), P("gy", "gz"), P()),
        out_specs=P("ka", None, None, "gy", "gz"),
        check_vma=False,
    )
```

time: 113 us -> 106 us (0.938)
  waiting for transfers between devices: 19.8 us -> 5.25 us
  starting transfers between devices: 14.6 us -> 23.9 us
  Pallas kernels: 64.7 us -> 60.4 us
  local copies, waits for them, and re-layouts: 4.46 us -> 7.55 us
    ppermute x6 -> x9, waiting for transfers between devices: 19.8 us -> 5.25 us  [the longest x6 3.9 us: shift(): return lax.ppermute(array, axis, pairs)]
    ppermute x6 -> x9, starting transfers between devices: 14.6 us -> 23.9 us  [the longest x6 20.3 us: shift(): return lax.ppermute(array, axis, pairs)]
    pallas_call x2, Pallas kernels: 64.7 us -> 60.4 us  [the longest x1 57.6 us: solve_field(): pl.pallas_call(functools.partial(field_kernel, sleepers, count, seglen, s...]
    slice x1 -> x5, local copies, waits for them, and re-layouts: 0.04 us -> 2.64 us  [the longest x1 1.06 us: local(): ends = jnp.concatenate([loads[:, :HB], loads[:, ny - HB:]], axis=1)]
  transfers between devices with their start and end apart: 6 -> 9, of which waited for: 4 -> 4; matrix products, arithmetic and copies ran while one was open for 9% -> 14% of each run, Pallas kernels for 0% -> 0%
where the time goes in v1:
time: 106 us
  Pallas kernels  60.4 us (57%)
  starting transfers between devices  23.9 us (23%)
  other arithmetic  8.16 us (8%)
  local copies, waits for them, and re-layouts  7.55 us (7%)
  waiting for transfers between devices  5.25 us (5%)
    pallas_call x1, Pallas kernels, solve_field(): pl.pallas_call(functools.partial(field_kernel, sleepers, count, seglen, s...  57.6 us
    ppermute x6, starting transfers between devices, shift(): return lax.ppermute(array, axis, pairs)  20.3 us
    ppermute x6, waiting for transfers between devices, shift(): return lax.ppermute(array, axis, pairs)  3.9 us
    pallas_call x1, Pallas kernels, edges_of(): pl.pallas_call(functools.partial(edge_kernel, sleepers, spots), out_shape...  2.71 us
    concatenate x1, other arithmetic, tables(): tw = jnp.concatenate([blocks(high), blocks(high), blocks(low)], axis=0)  2.21 us
  transfers between devices with their start and end apart: 9, of which 4 were waited for; matrix products, arithmetic and copies ran while one was open for 14% of the time, Pallas kernels for 0%

profile of v1, /device:TPU:1, one launch (start us, length us, event | category | flops | bytes accessed | tf_op | source)
XLA Modules:
  0.0 105.6 jit_solution(6246704531065630846)
XLA Ops:
  0.0 2.0 %collective-permute-start.2 = (s32[16]{0:T(128)}, s32[16]{0:T(128)S(1)}, u32[]{:S(2)}, u32[]{:S(2)}) collective-permute-start(s32[16]{0:T(128)} %param.5), channel_id=1, source_target_pairs={{0,16},{16,0},{1,17},{17,1},{2,18},{18,2},{3,19},{19,3},{4,20},{20... | collective-permute-start | bytes 200 | tf_op jit(solution)/shard_map/ppermute | solution.py:448
  2.0 0.7 convert_bitcast_fusion.refs_1_.refs_8_
  2.8 1.1 %fusion.11 = (f32[48,8,128]{2,1,0:T(8,128)S(1)}, f32[48,8,128]{2,1,0:T(8,128)S(1)}) fusion(f32[48,32,128]{2,1,0:T(8,128)} %bitcast.77), kind=kLoop, calls=%fused_computation.86 | loop fusion | bytes 786432 | tf_op jit(solution)/shard_map/slice | solution.py:444
  3.8 0.7 pad_maximum_fusion.2
  4.5 3.2 %collective-permute-start.3 = (f32[49,8,128]{2,1,0:T(8,128)}, f32[49,8,128]{2,1,0:T(8,128)S(1)}, u32[]{:S(2)}, u32[]{:S(2)}) collective-permute-start(f32[49,8,128]{2,1,0:T(8,128)} %pad_maximum_fusion.2), channel_id=1, source_target_pairs={{0,4},{4,8},{8,12},{1,5},{5,9},{9,13},{2,6},{6,10},{10,14},{3,7},{... | collective-permute-start | bytes 602120 | tf_op jit(solution)/shard_map/ppermute | solution.py:441
  7.7 0.7 pad_maximum_fusion.3
  8.4 1.3 %collective-permute-start.4 = (f32[49,8,128]{2,1,0:T(8,128)}, f32[49,8,128]{2,1,0:T(8,128)S(1)}, u32[]{:S(2)}, u32[]{:S(2)}) collective-permute-start(f32[49,8,128]{2,1,0:T(8,128)} %pad_maximum_fusion.3), channel_id=1, source_target_pairs={{4,0},{8,4},{12,8},{5,1},{9,5},{13,9},{6,2},{10,6},{14,10},{7,3},{... | collective-permute-start | bytes 602120 | tf_op jit(solution)/shard_map/ppermute | solution.py:441
  9.8 0.3 collective-permute-start
  10.1 0.8 slice.122
  10.8 1.2 %collective-permute-start.5 = (f32[48,16,128]{2,1,0:T(8,128)}, f32[48,16,128]{2,1,0:T(8,128)S(1)}, u32[]{:S(2)}, u32[]{:S(2)}) collective-permute-start(f32[48,16,128]{2,1,0:T(8,128)} %slice.122), channel_id=1, source_target_pairs={{0,16},{16,0},{1,17},{17,1},{2,18},{18,2},{3,19},{19,3},{4,20},{20... | collective-permute-start | bytes 1179656 | tf_op jit(solution)/shard_map/ppermute | solution.py:447
  12.2 0.3 slice_reduce_fusion
  14.0 0.4 multiply_convert_fusion
  14.6 0.2 copy.44
  14.8 0.6 add_convert_fusion.refs_0_
  15.5 0.6 pad_maximum_fusion.5.refs_6_
  16.1 0.9 pad.20.refs_4_
  17.8 1.3 %collective-permute-done.refs_4_.refs_11_ = f32[48,16,128]{2,1,0:T(8,128)S(1)} collective-permute-done((f32[48,16,128]{2,1,0:T(8,128)S(1)}, f32[48,16,128]{2,1,0:T(8,128)S(1)}, u32[]{:S(2)}, u32[]{:S(2)}) %collective-permute-start) | collective-permute-done | bytes 393248 | tf_op jit(solution)/shard_map/ppermute | solution.py:445
  19.2 0.8 fusion.13
  20.0 3.7 %collective-permute-start.6 = (f32[48,8,128]{2,1,0:T(8,128)S(1)}, f32[48,8,128]{2,1,0:T(8,128)S(1)}, u32[]{:S(2)}, u32[]{:S(2)}) collective-permute-start(f32[48,8,128]{2,1,0:T(8,128)S(1)} %get-tuple-element.35), channel_id=1, source_target_pairs={{0,4},{4,8},{8,12},{1,5},{5,9},{9,13},{2,6},{6,10},{10,14},{3,7},{... | collective-permute-start | bytes 589832 | tf_op jit(solution)/shard_map/ppermute | solution.py:441
  23.7 1.3 %collective-permute-start.1 = (f32[48,8,128]{2,1,0:T(8,128)}, f32[48,8,128]{2,1,0:T(8,128)S(1)}, u32[]{:S(2)}, u32[]{:S(2)}) collective-permute-start(f32[48,8,128]{2,1,0:T(8,128)} %get-tuple-element.36), channel_id=1, source_target_pairs={{4,0},{8,4},{12,8},{5,1},{9,5},{13,9},{6,2},{10,6},{14,10},{7,3},{... | collective-permute-start | bytes 589832 | tf_op jit(solution)/shard_map/ppermute | solution.py:441
  25.0 0.6 multiply_convert_fusion.2
  25.6 0.9 copy.35
  26.8 2.2 %pad_maximum_fusion.refs_3_ = bf16[768,768]{1,0:T(8,128)(2,1)} fusion(bf16[256,768]{1,0:T(8,128)(2,1)S(1)} %copy.37, bf16[256,768]{1,0:T(8,128)(2,1)} %copy.35), kind=kLoop, calls=%fused_computation | loop fusion | flops 3538944 | bytes 1966080 | tf_op jit(solution)/shard_map/concatenate | solution.py:83
  29.0 1.3 %collective-permute-done.1.refs_7_.refs_14_ = f32[48,8,128]{2,1,0:T(8,128)S(1)} collective-permute-done((f32[48,8,128]{2,1,0:T(8,128)}, f32[48,8,128]{2,1,0:T(8,128)S(1)}, u32[]{:S(2)}, u32[]{:S(2)}) %collective-permute-start.1) | collective-permute-done | bytes 196640 | tf_op jit(solution)/shard_map/ppermute | solution.py:441
  30.3 0.6 broadcast_in_dim.18.refs_5_
  31.0 2.7 %edge_columns.1 = f32[48,16,128]{2,1,0:T(8,128)S(1)} custom-call(f32[48,32,128]{2,1,0:T(8,128)S(1)} %bitcast.80, f32[1,32,128]{2,1,0:T(8,128)S(1)} %convert_bitcast_fusion.refs_1_.refs_8_, f32[49,8,128]{2,1,0:T(8,128)S(1)} %collective-permute-done.3.refs_2_.refs_9_, f32[49,8,128]{2,1,0:T(8,128)S(1)} %collective-permute-done.4.refs_3_.refs_10_, ...), custom_call_target="tpu_custom_call" | custom-call | tf_op jit(solution)/shard_map/edge_columns/pallas_call | solution.py:171
  33.8 7.8 %collective-permute-start.8 = (f32[48,8,128]{2,1,0:T(8,128)S(1)}, f32[48,8,128]{2,1,0:T(8,128)S(1)}, u32[]{:S(2)}, u32[]{:S(2)}) collective-permute-start(f32[48,8,128]{2,1,0:T(8,128)S(1)} %get-tuple-element.33), channel_id=1, source_target_pairs={{1,0},{2,1},{3,2},{5,4},{6,5},{7,6},{9,8},{10,9},{11,10},{13,12},{... | collective-permute-start | bytes 589832 | tf_op jit(solution)/shard_map/ppermute | solution.py:441
  41.6 3.0 %collective-permute-start.7 = (f32[48,8,128]{2,1,0:T(8,128)S(1)}, f32[48,8,128]{2,1,0:T(8,128)S(1)}, u32[]{:S(2)}, u32[]{:S(2)}) collective-permute-start(f32[48,8,128]{2,1,0:T(8,128)S(1)} %get-tuple-element.34), channel_id=1, source_target_pairs={{0,1},{1,2},{2,3},{4,5},{5,6},{6,7},{8,9},{9,10},{10,11},{12,13},{... | collective-permute-start | bytes 589832 | tf_op jit(solution)/shard_map/ppermute | solution.py:441
  44.7 1.4 %collective-permute-done.8.refs_2_ = f32[48,8,128]{2,1,0:T(8,128)S(1)} collective-permute-done((f32[48,8,128]{2,1,0:T(8,128)S(1)}, f32[48,8,128]{2,1,0:T(8,128)S(1)}, u32[]{:S(2)}, u32[]{:S(2)}) %collective-permute-start.8) | collective-permute-done | bytes 196640 | tf_op jit(solution)/shard_map/ppermute | solution.py:441
  46.1 1.2 %collective-permute-done.7.refs_1_ = f32[48,8,128]{2,1,0:T(8,128)S(1)} collective-permute-done((f32[48,8,128]{2,1,0:T(8,128)S(1)}, f32[48,8,128]{2,1,0:T(8,128)S(1)}, u32[]{:S(2)}, u32[]{:S(2)}) %collective-permute-start.7) | collective-permute-done | bytes 196640 | tf_op jit(solution)/shard_map/ppermute | solution.py:441
  47.3 0.7 copy-done.10
  48.0 57.6 %adjoint_field.1 = f32[64,2,3,32,128]{4,3,2,1,0:T(8,128)} custom-call(s32[2]{0:T(128)} %add_convert_fusion.refs_0_, f32[48,8,128]{2,1,0:T(8,128)} %copy-done.10, f32[48,8,128]{2,1,0:T(8,128)} %copy-done.9, bf16[768,768]{1,0:T(8,128)(2,1)} %pad_maximum_fusion.refs_3_, bf16[256,1024]{1,0:T(8,128)(2,1)} %pad.20.refs_4_, f32[4,8,128]{2,1,0:T(8,128)} %broadcast_in_dim.18.refs_5_, ...), custom_call_target="tpu_custom_call" | custom-call | tf_op jit(solution)/shard_map/adjoint_field/pallas_call | solution.py:400
  (76 shorter events, 2.8 us)
Async XLA Ops:
  0.0 10.1 %copy-start = (f32[16,3,32,128]{3,2,1,0:T(8,128)S(1)}, f32[16,3,32,128]{3,2,1,0:T(8,128)}, u32[]{:S(2)}) copy-start(f32[16,3,32,128]{3,2,1,0:T(8,128)} %param.4) | copy-start | bytes 2359300
  0.0 12.2 %copy-start.8 = (f32[8,8]{1,0:T(8,128)S(1)}, f32[8,8]{1,0:T(8,128)}, u32[]{:S(2)}) copy-start(f32[8,8]{1,0:T(8,128)} %param.7) | copy-start | bytes 772
  0.0 17.0 %collective-permute-start.2 = (s32[16]{0:T(128)}, s32[16]{0:T(128)S(1)}, u32[]{:S(2)}, u32[]{:S(2)}) collective-permute-start(s32[16]{0:T(128)} %param.5), channel_id=1, source_target_pairs={{0,16},{16,0},{1,17},{17,1},{2,18},{18,2},{3,19},{19,3},{4,20},{20... | collective-permute-start | bytes 200 | tf_op jit(solution)/shard_map/ppermute | solution.py:448
  2.8 28.2 %copy-start.7 = (f32[1,32,128]{2,1,0:T(8,128)}, f32[1,32,128]{2,1,0:T(8,128)S(1)}, u32[]{:S(2)}) copy-start(f32[1,32,128]{2,1,0:T(8,128)S(1)} %convert_bitcast_fusion.refs_1_.refs_8_) | copy-start | bytes 49156
  4.5 26.4 %collective-permute-start.3 = (f32[49,8,128]{2,1,0:T(8,128)}, f32[49,8,128]{2,1,0:T(8,128)S(1)}, u32[]{:S(2)}, u32[]{:S(2)}) collective-permute-start(f32[49,8,128]{2,1,0:T(8,128)} %pad_maximum_fusion.2), channel_id=1, source_target_pairs={{0,4},{4,8},{8,12},{1,5},{5,9},{9,13},{2,6},{6,10},{10,14},{3,7},{... | collective-permute-start | bytes 602120 | tf_op jit(solution)/shard_map/ppermute | solution.py:441
  8.4 22.5 %collective-permute-start.4 = (f32[49,8,128]{2,1,0:T(8,128)}, f32[49,8,128]{2,1,0:T(8,128)S(1)}, u32[]{:S(2)}, u32[]{:S(2)}) collective-permute-start(f32[49,8,128]{2,1,0:T(8,128)} %pad_maximum_fusion.3), channel_id=1, source_target_pairs={{4,0},{8,4},{12,8},{5,1},{9,5},{13,9},{6,2},{10,6},{14,10},{7,3},{... | collective-permute-start | bytes 602120 | tf_op jit(solution)/shard_map/ppermute | solution.py:441
  9.8 9.4 %collective-permute-start = (f32[48,16,128]{2,1,0:T(8,128)S(1)}, f32[48,16,128]{2,1,0:T(8,128)S(1)}, u32[]{:S(2)}, u32[]{:S(2)}) collective-permute-start(f32[48,16,128]{2,1,0:T(8,128)S(1)} %pad_maximum_fusion.1), channel_id=1, source_target_pairs={{0,16},{16,0},{1,17},{17,1},{2,18},{18,2},{3,19},{19,3},{4,20},{20... | collective-permute-start | bytes 1179656 | tf_op jit(solution)/shard_map/ppermute | solution.py:445
  10.8 20.1 %collective-permute-start.5 = (f32[48,16,128]{2,1,0:T(8,128)}, f32[48,16,128]{2,1,0:T(8,128)S(1)}, u32[]{:S(2)}, u32[]{:S(2)}) collective-permute-start(f32[48,16,128]{2,1,0:T(8,128)} %slice.122), channel_id=1, source_target_pairs={{0,16},{16,0},{1,17},{17,1},{2,18},{18,2},{3,19},{19,3},{4,20},{20... | collective-permute-start | bytes 1179656 | tf_op jit(solution)/shard_map/ppermute | solution.py:447
  13.0 4.1 %copy-start.11 = (s32[16]{0:T(128)S(1)}, s32[16]{0:T(128)}, u32[]{:S(2)}) copy-start(s32[16]{0:T(128)} %param.5) | copy-start | bytes 196
  19.2 11.8 %copy-start.1 = (f32[48,16,128]{2,1,0:T(8,128)}, f32[48,16,128]{2,1,0:T(8,128)S(1)}, u32[]{:S(2)}) copy-start(f32[48,16,128]{2,1,0:T(8,128)S(1)} %collective-permute-done.refs_4_.refs_11_) | copy-start | bytes 1179652
  20.0 11.0 %collective-permute-start.6 = (f32[48,8,128]{2,1,0:T(8,128)S(1)}, f32[48,8,128]{2,1,0:T(8,128)S(1)}, u32[]{:S(2)}, u32[]{:S(2)}) collective-permute-start(f32[48,8,128]{2,1,0:T(8,128)S(1)} %get-tuple-element.35), channel_id=1, source_target_pairs={{0,4},{4,8},{8,12},{1,5},{5,9},{9,13},{2,6},{6,10},{10,14},{3,7},{... | collective-permute-start | bytes 589832 | tf_op jit(solution)/shard_map/ppermute | solution.py:441
  23.7 6.6 %collective-permute-start.1 = (f32[48,8,128]{2,1,0:T(8,128)}, f32[48,8,128]{2,1,0:T(8,128)S(1)}, u32[]{:S(2)}, u32[]{:S(2)}) collective-permute-start(f32[48,8,128]{2,1,0:T(8,128)} %get-tuple-element.36), channel_id=1, source_target_pairs={{4,0},{8,4},{12,8},{5,1},{9,5},{13,9},{6,2},{10,6},{14,10},{7,3},{... | collective-permute-start | bytes 589832 | tf_op jit(solution)/shard_map/ppermute | solution.py:441
  30.3 16.9 %copy-start.6 = (f32[48,8,128]{2,1,0:T(8,128)}, f32[48,8,128]{2,1,0:T(8,128)S(1)}, u32[]{:S(2)}) copy-start(f32[48,8,128]{2,1,0:T(8,128)S(1)} %collective-permute-done.1.refs_7_.refs_14_) | copy-start | bytes 589828
  30.9 16.3 %copy-start.3 = (f32[49,8,128]{2,1,0:T(8,128)}, f32[49,8,128]{2,1,0:T(8,128)S(1)}, u32[]{:S(2)}) copy-start(f32[49,8,128]{2,1,0:T(8,128)S(1)} %collective-permute-done.3.refs_2_.refs_9_) | copy-start | bytes 602116
  30.9 16.3 %copy-start.4 = (f32[49,8,128]{2,1,0:T(8,128)}, f32[49,8,128]{2,1,0:T(8,128)S(1)}, u32[]{:S(2)}) copy-start(f32[49,8,128]{2,1,0:T(8,128)S(1)} %collective-permute-done.4.refs_3_.refs_10_) | copy-start | bytes 602116
  31.0 16.3 %copy-start.2 = (f32[48,16,128]{2,1,0:T(8,128)}, f32[48,16,128]{2,1,0:T(8,128)S(1)}, u32[]{:S(2)}) copy-start(f32[48,16,128]{2,1,0:T(8,128)S(1)} %collective-permute-done.5.refs_5_.refs_12_) | copy-start | bytes 1179652
  31.0 16.3 %copy-start.5 = (f32[48,8,128]{2,1,0:T(8,128)}, f32[48,8,128]{2,1,0:T(8,128)S(1)}, u32[]{:S(2)}) copy-start(f32[48,8,128]{2,1,0:T(8,128)S(1)} %collective-permute-done.6.refs_6_.refs_13_) | copy-start | bytes 589828
  33.8 12.3 %collective-permute-start.8 = (f32[48,8,128]{2,1,0:T(8,128)S(1)}, f32[48,8,128]{2,1,0:T(8,128)S(1)}, u32[]{:S(2)}, u32[]{:S(2)}) collective-permute-start(f32[48,8,128]{2,1,0:T(8,128)S(1)} %get-tuple-element.33), channel_id=1, source_target_pairs={{1,0},{2,1},{3,2},{5,4},{6,5},{7,6},{9,8},{10,9},{11,10},{13,12},{... | collective-permute-start | bytes 589832 | tf_op jit(solution)/shard_map/ppermute | solution.py:441
  41.6 5.6 %collective-permute-start.7 = (f32[48,8,128]{2,1,0:T(8,128)S(1)}, f32[48,8,128]{2,1,0:T(8,128)S(1)}, u32[]{:S(2)}, u32[]{:S(2)}) collective-permute-start(f32[48,8,128]{2,1,0:T(8,128)S(1)} %get-tuple-element.34), channel_id=1, source_target_pairs={{0,1},{1,2},{2,3},{4,5},{5,6},{6,7},{8,9},{9,10},{10,11},{12,13},{... | collective-permute-start | bytes 589832 | tf_op jit(solution)/shard_map/ppermute | solution.py:441
  46.1 1.2 %copy-start.9 = (f32[48,8,128]{2,1,0:T(8,128)}, f32[48,8,128]{2,1,0:T(8,128)S(1)}, u32[]{:S(2)}) copy-start(f32[48,8,128]{2,1,0:T(8,128)S(1)} %collective-permute-done.8.refs_2_) | copy-start | bytes 589828
  47.3 0.7 copy-start.10
